TPU v7x, 256 devices: a whole 4x4x8 slice. The times are simulated.
256 devices in a mesh: gx: 8 (over z_hi, y), gy: 32 (over x, z_lo, core).
Axes of the slice: x: 4, y: 4, z: 8 (z_hi: 2, z_lo: 4; z = z_hi * 4 + z_lo), core: 2. Of those that a mesh axis runs over, the one named last changes fastest.
Arguments:
- density: float32 [2, 2048, 8192], P(None, 'gx', 'gy'), may hold values from -6 to 6
- observed: float32 [2048, 8192], P('gx', 'gy'), may hold values from -6 to 6
- stations: int32 [2048, 8192], P('gx', 'gy'), may hold values 0 or 1
- layer_index: int32 [2], replicated, may hold values from 0 to 511
Outputs:
- predicted: float32 [2048, 8192], P('gx', 'gy')
- residual: float32 [2048, 8192], P('gx', 'gy')
- gradient: float32 [2, 2048, 8192], P(None, 'gx', 'gy')
All inputs are finite; a program needn't handle non-finite values. No bound on the sum of `stations` on one device may be relied on, other than what follows from the above.
Results may differ from a plain program's by a relative error of at most 0.00016.
Values sent between devices are 32-bit elements; how exact they have to be, the bound alone decides.
A program may use at most 64 MiB of HBM per device.

v0:
```python
import functools
import math

import jax
import jax.numpy as jnp
import numpy as np
from jax import lax
from jax.experimental import pallas as pl
from jax.experimental.pallas import tpu as pltpu
from jax.sharding import PartitionSpec as P

RADIUS = 128
LAYERS_ALL = 512
MESH = pl.DeviceIdType.MESH
F32 = jnp.float32
BF16 = jnp.bfloat16

DIRS = ((1, 0), (-1, 0), (1, 1), (1, -1), (-1, 1), (-1, -1), (0, 1), (0, -1))


def halves(table):
    high = table.astype(BF16)
    return high, (table - high.astype(np.float64)).astype(BF16)


def tables(length):
    half = length // 2
    odd = 2 * np.arange(half)[:, None] + 1
    phase = (odd * (2 * np.arange(length)[None, :] - length + 1)) % (4 * length)
    angle = phase * (2.0 * math.pi / (4 * length))
    basis = np.concatenate([np.cos(angle), np.sin(angle)])
    ticks = np.arange(half)[None, :]
    kphase = (odd * ticks) % (2 * length)
    weight = np.where(ticks == 0, 1.0, 2.0) * (ticks <= RADIUS) / half
    cosines = np.cos(kphase * (2.0 * math.pi / (2 * length))) * weight
    return halves(basis), halves(np.ascontiguousarray(basis.T)), halves(cosines)


def dot(left, right):
    return lax.dot_general(left, right, (((1,), (0,)), ((), ())), preferred_element_type=F32)


def dot_t(left, right):
    return lax.dot_general(left, right, (((1,), (1,)), ((), ())), preferred_element_type=F32)


def split(value):
    high = value.astype(BF16)
    return high, (value - high.astype(F32)).astype(BF16)


def product(left, right, how=dot):
    return how(left[0], right[0]) + (how(left[1], right[0]) + how(left[0], right[1]))


def part(refs, rows, cols):
    return refs[0][rows, cols], refs[1][rows, cols]


def put(refs, rows, cols, value):
    refs[0][rows, cols], refs[1][rows, cols] = split(value)


def forward_kernel(
    counts,
    index, density, observed, stations, bas_h, bas_l, tra_h, tra_l, cos_h, cos_l,
    predicted, residual, blocks, spectra,
    den, obs, sta, b_h, b_l, t_h, t_l, c_h, c_l,
    s_h, s_l, z_h, z_l, total, big, win, from_x, from_y, from_d,
    load_sem, send_sem, recv_sem,
):
    gx, gy = lax.axis_index("gx"), lax.axis_index("gy")
    nx, ny = counts
    layers, tile = den.shape[0], den.shape[1]
    length = tile + 2 * RADIUS
    half = length // 2
    low, mid, high = slice(0, RADIUS), slice(RADIUS, RADIUS + tile), slice(RADIUS + tile, length)
    first, last = slice(RADIUS, 2 * RADIUS), slice(tile, RADIUS + tile)
    every = slice(0, length)

    def there(dx, dy):
        conds = []
        if dx:
            conds.append(gx < nx - 1 if dx > 0 else gx > 0)
        if dy:
            conds.append(gy < ny - 1 if dy > 0 else gy > 0)
        return functools.reduce(jnp.logical_and, conds)

    def target(dx, dy):
        return {"gx": gx + dx, "gy": gy + dy}

    barrier = pltpu.get_barrier_semaphore()
    for dx, dy in DIRS:
        @pl.when(there(dx, dy))
        def _(dx=dx, dy=dy):
            pl.semaphore_signal(barrier, inc=1, device_id=target(dx, dy), device_id_type=MESH)

    pairs = ((cos_h, c_h), (cos_l, c_l), (density, den), (tra_h, t_h), (tra_l, t_l), (bas_h, b_h), (bas_l, b_l), (observed, obs), (stations, sta))
    loads = [pltpu.make_async_copy(src, dst, load_sem.at[i]) for i, (src, dst) in enumerate(pairs)]
    for load in loads:
        load.start()

    @pl.when(gx == 0)
    def _():
        win[low, :] = jnp.zeros((RADIUS, length), F32)

    @pl.when(gx == nx - 1)
    def _():
        win[high, :] = jnp.zeros((RADIUS, length), F32)

    @pl.when(gy == 0)
    def _():
        win[:, low] = jnp.zeros((length, RADIUS), F32)

    @pl.when(gy == ny - 1)
    def _():
        win[:, high] = jnp.zeros((length, RADIUS), F32)

    rows = lax.broadcasted_iota(jnp.int32, (half, half), 0).astype(F32)
    cols = lax.broadcasted_iota(jnp.int32, (half, half), 1).astype(F32)
    flat = rows * rows + cols * cols
    loads[0].wait()
    loads[1].wait()
    cosines = (c_h[...], c_l[...])
    for layer in range(layers):
        depth = RADIUS * (0.375 + index[layer].astype(F32) / LAYERS_ALL)
        square = flat + depth * depth
        inverse = lax.rsqrt(square)
        value = (depth * depth) * (inverse * inverse * inverse)
        left = product(cosines, split(value))
        spectra[layer] = product(split(left), cosines, dot_t)

    for load in loads[2:7]:
        load.wait()
    basis, trans = (b_h, b_l), (t_h, t_l)
    for layer in range(layers):
        put((s_h, s_l), slice(0, tile), every, product(split(den[layer]), part(trans, mid, every)))
        spectrum = spectra[layer]
        for r in range(2):
            band = slice(r * half, (r + 1) * half)
            out = product(part(basis, band, mid), part((s_h, s_l), slice(0, tile), every))
            for c in range(2):
                at = slice(c * half, (c + 1) * half)
                term = spectrum * out[:, at]
                total[band, at] = term if layer == 0 else total[band, at] + term
    for r in range(2):
        band = slice(r * half, (r + 1) * half)
        put((z_h, z_l), band, every, total[band, :])
    for r in range(2):
        band = slice(r * half, (r + 1) * half)
        put((s_h, s_l), band, every, product(part((z_h, z_l), band, every), part(basis, every, every)))

    def pieces(dx, dy):
        rs = {1: high, -1: low, 0: mid}[dx]
        cs = {1: high, -1: low, 0: mid}[dy]
        if dx and dy:
            return big.at[rs, cs], from_d.at[(dx < 0) * 2 + (dy < 0)]
        if dx:
            return big.at[rs, cs], from_x.at[int(dx < 0)]
        return big.at[rs, cs], from_y.at[int(dy < 0)]

    def fold_copy(k):
        dx, dy = DIRS[k]
        src, dst = pieces(dx, dy)
        return pltpu.make_async_remote_copy(
            src_ref=src, dst_ref=dst, send_sem=send_sem.at[0, k], recv_sem=recv_sem.at[0, k],
            device_id=target(dx, dy), device_id_type=MESH,
        )

    def halo_copy(k):
        dx, dy = DIRS[k]
        near, far = {1: last, -1: first, 0: mid}, {1: low, -1: high, 0: mid}
        return pltpu.make_async_remote_copy(
            src_ref=win.at[near[dx], near[dy]], dst_ref=win.at[far[dx], far[dy]],
            send_sem=send_sem.at[1, k], recv_sem=recv_sem.at[1, k],
            device_id=target(dx, dy), device_id_type=MESH,
        )

    def start(make, ks):
        for k in ks:
            @pl.when(there(*DIRS[k]))
            def _(k=k):
                make(k).start()

    def sent(make):
        for k in range(8):
            @pl.when(there(*DIRS[k]))
            def _(k=k):
                make(k).wait_send()

    def received(make, ks, then=None):
        for k in ks:
            dx, dy = DIRS[k]
            @pl.when(there(-dx, -dy))
            def _(k=k):
                make(k).wait_recv()
                if then is not None:
                    then(k)

    sides_x = 2 - (gx == 0).astype(jnp.int32) - (gx == nx - 1).astype(jnp.int32)
    sides_y = 2 - (gy == 0).astype(jnp.int32) - (gy == ny - 1).astype(jnp.int32)
    pl.semaphore_wait(barrier, (sides_x + 1) * (sides_y + 1) - 1)

    def back(rs, cs):
        big[rs, cs] = product(part(trans, rs, every), part((s_h, s_l), every, cs))

    back(high, every)
    start(fold_copy, (0, 2, 3))
    back(low, every)
    start(fold_copy, (1, 4, 5))
    back(mid, every)
    start(fold_copy, (6, 7))
    for load in loads[7:]:
        load.wait()

    def fold(k):
        dx, dy = DIRS[k]
        rs = {1: first, -1: last, 0: mid}[dx]
        cs = {1: first, -1: last, 0: mid}[dy]
        big[rs, cs] = big[rs, cs] + pieces(dx, dy)[1][...]

    received(fold_copy, (6, 7, 0, 1, 2, 3, 4, 5), fold)
    total_pred = big[mid, mid]
    misfit = sta[...].astype(F32) * (total_pred - obs[...])
    win[mid, mid] = misfit
    start(halo_copy, range(8))
    predicted[...] = total_pred
    residual[...] = misfit

    received(halo_copy, (6, 7))
    put((s_h, s_l), slice(0, tile), every, product(split(win[mid, :]), part(trans, every, every)))
    for r in range(2):
        band = slice(r * half, (r + 1) * half)
        total[band, :] = product(part(basis, band, mid), part((s_h, s_l), slice(0, tile), every))

    received(halo_copy, range(6))
    put((s_h, s_l), low, every, product(split(win[low, :]), part(trans, every, every)))
    put((s_h, s_l), high, every, product(split(win[high, :]), part(trans, every, every)))
    for r in range(2):
        band = slice(r * half, (r + 1) * half)
        blocks[band, :] = (
            total[band, :]
            + product(part(basis, band, low), part((s_h, s_l), low, every))
            + product(part(basis, band, high), part((s_h, s_l), high, every))
        )
    sent(fold_copy)
    sent(halo_copy)


def adjoint_kernel(
    predicted, residual, blocks, spectra, bas_h, bas_l, tra_h, tra_l,
    predicted_out, residual_out, gradient,
    b_h, b_l, t_h, t_l, z_h, z_l, w_h, w_l, grad, load_sem, out_sem,
):
    layers, tile = spectra.shape[0], residual.shape[0]
    length = tile + 2 * RADIUS
    half = length // 2
    mid = slice(RADIUS, RADIUS + tile)
    every = slice(0, length)
    loads = [
        pltpu.make_async_copy(bas_h.at[:, mid], b_h, load_sem.at[0]),
        pltpu.make_async_copy(bas_l.at[:, mid], b_l, load_sem.at[1]),
        pltpu.make_async_copy(tra_h.at[mid, :], t_h, load_sem.at[2]),
        pltpu.make_async_copy(tra_l.at[mid, :], t_l, load_sem.at[3]),
    ]
    for load in loads:
        load.start()
    stores = [
        pltpu.make_async_copy(predicted, predicted_out, out_sem.at[0]),
        pltpu.make_async_copy(residual, residual_out, out_sem.at[1]),
    ]
    for store in stores:
        store.start()
    for load in loads:
        load.wait()
    for layer in range(layers):
        spectrum = spectra[layer]
        for r in range(2):
            band = slice(r * half, (r + 1) * half)
            for c in range(2):
                at = slice(c * half, (c + 1) * half)
                put((z_h, z_l), band, at, spectrum * blocks[band, at])
        for r in range(2):
            band = slice(r * half, (r + 1) * half)
            put((w_h, w_l), band, slice(0, tile), product(part((z_h, z_l), band, every), (b_h[...], b_l[...])))
        grad[layer] = product((t_h[...], t_l[...]), (w_h[...], w_l[...]))
        store = pltpu.make_async_copy(grad.at[layer], gradient.at[layer], out_sem.at[2 + layer])
        store.start()
        stores.append(store)
    for store in stores:
        store.wait()


def solution(mesh):
    counts = (mesh.shape["gx"], mesh.shape["gy"])

    def body(density, observed, stations, layer_index):
        layers, tile = density.shape[0], density.shape[1]
        length = tile + 2 * RADIUS
        half = length // 2
        (bas_h, bas_l), (tra_h, tra_l), (cos_h, cos_l) = tables(length)
        anywhere = pl.BlockSpec(memory_space=pl.ANY)
        vmem = pl.BlockSpec(memory_space=pltpu.VMEM)
        big = pltpu.VMEM((length, length), F32)
        wide = pltpu.VMEM((length, length), BF16)
        small = pltpu.VMEM((half, half), BF16)
        predicted, residual, blocks, spectra = pl.pallas_call(
            functools.partial(forward_kernel, counts),
            out_shape=(
                pltpu.VMEM((tile, tile), F32),
                pltpu.VMEM((tile, tile), F32),
                pltpu.VMEM((length, length), F32),
                pltpu.VMEM((layers, half, half), F32),
            ),
            in_specs=[pl.BlockSpec(memory_space=pltpu.SMEM)] + [anywhere] * 9,
            out_specs=(vmem,) * 4,
            scratch_shapes=[
                pltpu.VMEM(density.shape, F32),
                pltpu.VMEM((tile, tile), F32),
                pltpu.VMEM((tile, tile), jnp.int32),
                wide, wide, wide, wide, small, small,
                wide, wide, wide, wide, big, big, big,
                pltpu.VMEM((2, RADIUS, tile), F32),
                pltpu.VMEM((2, tile, RADIUS), F32),
                pltpu.VMEM((4, RADIUS, RADIUS), F32),
                pltpu.SemaphoreType.DMA((9,)),
                pltpu.SemaphoreType.DMA((2, 8)),
                pltpu.SemaphoreType.DMA((2, 8)),
            ],
            compiler_params=pltpu.CompilerParams(
                collective_id=0, has_side_effects=True, vmem_limit_bytes=32 << 20
            ),
            name="forward",
        )(layer_index, density, observed, stations, bas_h, bas_l, tra_h, tra_l, cos_h, cos_l)
        return pl.pallas_call(
            adjoint_kernel,
            out_shape=(
                jax.ShapeDtypeStruct((tile, tile), F32),
                jax.ShapeDtypeStruct((tile, tile), F32),
                jax.ShapeDtypeStruct((layers, tile, tile), F32),
            ),
            in_specs=[vmem] * 4 + [anywhere] * 4,
            out_specs=(anywhere,) * 3,
            scratch_shapes=[
                pltpu.VMEM((length, tile), BF16),
                pltpu.VMEM((length, tile), BF16),
                pltpu.VMEM((tile, length), BF16),
                pltpu.VMEM((tile, length), BF16),
                wide, wide,
                pltpu.VMEM((length, tile), BF16),
                pltpu.VMEM((length, tile), BF16),
                pltpu.VMEM((layers, tile, tile), F32),
                pltpu.SemaphoreType.DMA((4,)),
                pltpu.SemaphoreType.DMA((2 + layers,)),
            ],
            compiler_params=pltpu.CompilerParams(vmem_limit_bytes=24 << 20),
            name="adjoint",
        )(predicted, residual, blocks, spectra, bas_h, bas_l, tra_h, tra_l)

    in_specs = (P(None, "gx", "gy"), P("gx", "gy"), P("gx", "gy"), P())
    out_specs = (P("gx", "gy"), P("gx", "gy"), P(None, "gx", "gy"))
    return jax.shard_map(body, mesh=mesh, in_specs=in_specs, out_specs=out_specs, check_vma=False)
```

profile of v0, /device:TPU:60, one launch (start us, length us, event | category | flops | bytes accessed | tf_op | source)
XLA Modules:
  0.0 57.3 jit_solution(8605157637653183123)
XLA Ops:
  0.6 0.0 copy-start
  0.6 1.0 %copy-done = bf16[512,512]{1,0:T(8,128)(2,1)S(1)} copy-done((bf16[512,512]{1,0:T(8,128)(2,1)S(1)}, bf16[512,512]{1,0:T(8,128)(2,1)}, u32[]{:S(2)}) %copy-start) | copy-done | bytes 524312
  1.7 0.0 copy-start.1
  1.7 1.0 %copy-done.1 = bf16[512,512]{1,0:T(8,128)(2,1)S(1)} copy-done((bf16[512,512]{1,0:T(8,128)(2,1)S(1)}, bf16[512,512]{1,0:T(8,128)(2,1)}, u32[]{:S(2)}) %copy-start.1) | copy-done | bytes 524312
  2.7 0.0 copy-start.2
  2.7 1.0 %copy-done.2 = bf16[512,512]{1,0:T(8,128)(2,1)S(1)} copy-done((bf16[512,512]{1,0:T(8,128)(2,1)S(1)}, bf16[512,512]{1,0:T(8,128)(2,1)}, u32[]{:S(2)}) %copy-start.2) | copy-done | bytes 524312
  3.8 0.0 copy-start.3
  3.8 1.0 %copy-done.3 = bf16[512,512]{1,0:T(8,128)(2,1)S(1)} copy-done((bf16[512,512]{1,0:T(8,128)(2,1)S(1)}, bf16[512,512]{1,0:T(8,128)(2,1)}, u32[]{:S(2)}) %copy-start.3) | copy-done | bytes 524312
  4.8 0.0 copy-start.4
  4.8 1.0 %copy-done.4 = f32[2,256,256]{2,1,0:T(8,128)S(1)} copy-done((f32[2,256,256]{2,1,0:T(8,128)S(1)}, f32[2,256,256]{2,1,0:T(8,128)}, u32[]{:S(2)}) %copy-start.4) | copy-done | bytes 524312
  5.8 0.0 copy-start.5
  5.8 0.9 %copy-done.5 = f32[256,256]{1,0:T(8,128)S(1)} copy-done((f32[256,256]{1,0:T(8,128)S(1)}, f32[256,256]{1,0:T(8,128)}, u32[]{:S(2)}) %copy-start.5) | copy-done | bytes 262168
  6.8 0.0 copy-start.6
  6.8 0.9 %copy-done.6 = s32[256,256]{1,0:T(8,128)S(1)} copy-done((s32[256,256]{1,0:T(8,128)S(1)}, s32[256,256]{1,0:T(8,128)}, u32[]{:S(2)}) %copy-start.6) | copy-done | bytes 262168
  7.7 0.0 copy-start.7
  7.7 0.9 %copy-done.7 = bf16[256,256]{1,0:T(8,128)(2,1)S(1)} copy-done((bf16[256,256]{1,0:T(8,128)(2,1)S(1)}, bf16[256,256]{1,0:T(8,128)(2,1)}, u32[]{:S(2)}) %copy-start.7) | copy-done | bytes 131096
  8.7 0.0 copy-start.8
  8.7 0.9 %copy-done.8 = bf16[256,256]{1,0:T(8,128)(2,1)S(1)} copy-done((bf16[256,256]{1,0:T(8,128)(2,1)S(1)}, bf16[256,256]{1,0:T(8,128)(2,1)}, u32[]{:S(2)}) %copy-start.8) | copy-done | bytes 131096
  9.6 0.0 copy-start.9
  9.6 0.7 %copy-done.9 = s32[2]{0:T(128)S(1)} copy-done((s32[2]{0:T(128)S(1)}, s32[2]{0:T(128)}, u32[]{:S(2)}) %copy-start.9) | copy-done | bytes 32
  10.2 44.2 %forward.1 = (f32[256,256]{1,0:T(8,128)S(1)}, f32[256,256]{1,0:T(8,128)S(1)}, f32[512,512]{1,0:T(8,128)S(1)}, f32[2,256,256]{2,1,0:T(8,128)S(1)}) custom-call(s32[2]{0:T(128)S(1)} %copy-done.9, f32[2,256,256]{2,1,0:T(8,128)S(1)} %copy-done.4, f32[256,256]{1,0:T(8,128)S(1)} %copy-done.5, s32[256,256]{1,0:T(8,128)S(1)} %copy-done.6, ...), custom_call_target="tpu_custom_call" | custom-call | tf_op jit(solution)/shard_map/forward/pallas_call | solution.py:307
  54.4 2.9 %adjoint.1 = (f32[256,256]{1,0:T(8,128)}, f32[256,256]{1,0:T(8,128)}, f32[2,256,256]{2,1,0:T(8,128)}) custom-call(f32[256,256]{1,0:T(8,128)S(1)} %get-tuple-element.7.predicted, f32[256,256]{1,0:T(8,128)S(1)} %get-tuple-element.8.residual, f32[512,512]{1,0:T(8,128)S(1)} %get-tuple-element.9.blocks, f32[2,256,256]{2,1,0:T(8,128)S(1)} %get-tuple-element.10.spectra, ...), custom_call_target="tpu_custom_call" | custom-call | tf_op jit(solution)/shard_map/adjoint/pallas_call | solution.py:335
Async XLA Ops:
  0.6 1.0 %copy-start = (bf16[512,512]{1,0:T(8,128)(2,1)S(1)}, bf16[512,512]{1,0:T(8,128)(2,1)}, u32[]{:S(2)}) copy-start(bf16[512,512]{1,0:T(8,128)(2,1)} %constant.15.clone.tra_l) | copy-start | bytes 1572868
  1.7 1.0 %copy-start.1 = (bf16[512,512]{1,0:T(8,128)(2,1)S(1)}, bf16[512,512]{1,0:T(8,128)(2,1)}, u32[]{:S(2)}) copy-start(bf16[512,512]{1,0:T(8,128)(2,1)} %constant.14.clone.tra_h) | copy-start | bytes 1572868
  2.7 1.0 %copy-start.2 = (bf16[512,512]{1,0:T(8,128)(2,1)S(1)}, bf16[512,512]{1,0:T(8,128)(2,1)}, u32[]{:S(2)}) copy-start(bf16[512,512]{1,0:T(8,128)(2,1)} %constant.13.clone.bas_l) | copy-start | bytes 1572868
  3.8 1.0 %copy-start.3 = (bf16[512,512]{1,0:T(8,128)(2,1)S(1)}, bf16[512,512]{1,0:T(8,128)(2,1)}, u32[]{:S(2)}) copy-start(bf16[512,512]{1,0:T(8,128)(2,1)} %constant.12.clone.bas_h) | copy-start | bytes 1572868
  4.8 1.0 %copy-start.4 = (f32[2,256,256]{2,1,0:T(8,128)S(1)}, f32[2,256,256]{2,1,0:T(8,128)}, u32[]{:S(2)}) copy-start(f32[2,256,256]{2,1,0:T(8,128)} %density.1) | copy-start | bytes 1572868
  5.8 0.9 %copy-start.5 = (f32[256,256]{1,0:T(8,128)S(1)}, f32[256,256]{1,0:T(8,128)}, u32[]{:S(2)}) copy-start(f32[256,256]{1,0:T(8,128)} %observed.1) | copy-start | bytes 786436
  6.8 0.9 %copy-start.6 = (s32[256,256]{1,0:T(8,128)S(1)}, s32[256,256]{1,0:T(8,128)}, u32[]{:S(2)}) copy-start(s32[256,256]{1,0:T(8,128)} %stations.1) | copy-start | bytes 786436
  7.7 0.9 %copy-start.7 = (bf16[256,256]{1,0:T(8,128)(2,1)S(1)}, bf16[256,256]{1,0:T(8,128)(2,1)}, u32[]{:S(2)}) copy-start(bf16[256,256]{1,0:T(8,128)(2,1)} %constant.17.clone.cos_l) | copy-start | bytes 393220
  8.7 0.9 %copy-start.8 = (bf16[256,256]{1,0:T(8,128)(2,1)S(1)}, bf16[256,256]{1,0:T(8,128)(2,1)}, u32[]{:S(2)}) copy-start(bf16[256,256]{1,0:T(8,128)(2,1)} %constant.16.clone.cos_h) | copy-start | bytes 393220
  9.6 0.7 %copy-start.9 = (s32[2]{0:T(128)S(1)}, s32[2]{0:T(128)}, u32[]{:S(2)}) copy-start(s32[2]{0:T(128)} %index.1) | copy-start | bytes 28
where the time goes:
time: 57.7 us; the launch traced here: 57.3 us
  Pallas kernels  47.1 us (82%)
  local copies, waits for them, and re-layouts  9.56 us (17%)
  between operations  0.66 us (1%)
    pallas_call x1, Pallas kernels, body(): pl.pallas_call(functools.partial(forward_kernel, counts), out_shape=(pltp...  44.2 us
    unnamed x20, local copies, waits for them, and re-layouts  9.56 us
    pallas_call x1, Pallas kernels, body(): pl.pallas_call(adjoint_kernel, out_shape=(jax.ShapeDtypeStruct((tile, til...  2.87 us

commit v1 on v0

--- a/solution.py
+++ b/solution.py
@@ -44,6 +44,10 @@
     return lax.dot_general(left, right, (((1,), (1,)), ((), ())), preferred_element_type=F32)
 
 
+def in_hbm(array):
+    return pltpu.with_memory_space_constraint(array, pltpu.HBM)
+
+
 def split(value):
     high = value.astype(BF16)
     return high, (value - high.astype(F32)).astype(BF16)
@@ -63,11 +67,11 @@
 
 def forward_kernel(
     counts,
-    index, density, observed, stations, bas_h, bas_l, tra_h, tra_l, cos_h, cos_l,
+    layer_index, density, observed, stations, bas_h, bas_l, tra_h, tra_l, cos_h, cos_l,
     predicted, residual, blocks, spectra,
     den, obs, sta, b_h, b_l, t_h, t_l, c_h, c_l,
     s_h, s_l, z_h, z_l, total, big, win, from_x, from_y, from_d,
-    load_sem, send_sem, recv_sem,
+    index, index_sem, load_sem, send_sem, recv_sem,
 ):
     gx, gy = lax.axis_index("gx"), lax.axis_index("gy")
     nx, ny = counts
@@ -97,6 +101,8 @@
 
     pairs = ((cos_h, c_h), (cos_l, c_l), (density, den), (tra_h, t_h), (tra_l, t_l), (bas_h, b_h), (bas_l, b_l), (observed, obs), (stations, sta))
     loads = [pltpu.make_async_copy(src, dst, load_sem.at[i]) for i, (src, dst) in enumerate(pairs)]
+    index_load = pltpu.make_async_copy(layer_index, index, index_sem)
+    index_load.start()
     for load in loads:
         load.start()
 
@@ -119,6 +125,7 @@
     rows = lax.broadcasted_iota(jnp.int32, (half, half), 0).astype(F32)
     cols = lax.broadcasted_iota(jnp.int32, (half, half), 1).astype(F32)
     flat = rows * rows + cols * cols
+    index_load.wait()
     loads[0].wait()
     loads[1].wait()
     cosines = (c_h[...], c_l[...])
@@ -312,7 +319,7 @@
                 pltpu.VMEM((length, length), F32),
                 pltpu.VMEM((layers, half, half), F32),
             ),
-            in_specs=[pl.BlockSpec(memory_space=pltpu.SMEM)] + [anywhere] * 9,
+            in_specs=[anywhere] * 10,
             out_specs=(vmem,) * 4,
             scratch_shapes=[
                 pltpu.VMEM(density.shape, F32),
@@ -323,6 +330,8 @@
                 pltpu.VMEM((2, RADIUS, tile), F32),
                 pltpu.VMEM((2, tile, RADIUS), F32),
                 pltpu.VMEM((4, RADIUS, RADIUS), F32),
+                pltpu.SMEM((layers,), jnp.int32),
+                pltpu.SemaphoreType.DMA,
                 pltpu.SemaphoreType.DMA((9,)),
                 pltpu.SemaphoreType.DMA((2, 8)),
                 pltpu.SemaphoreType.DMA((2, 8)),
@@ -331,7 +340,7 @@
                 collective_id=0, has_side_effects=True, vmem_limit_bytes=32 << 20
             ),
             name="forward",
-        )(layer_index, density, observed, stations, bas_h, bas_l, tra_h, tra_l, cos_h, cos_l)
+        )(*map(in_hbm, (layer_index, density, observed, stations, bas_h, bas_l, tra_h, tra_l, cos_h, cos_l)))
         return pl.pallas_call(
             adjoint_kernel,
             out_shape=(
@@ -355,7 +364,7 @@
             ],
             compiler_params=pltpu.CompilerParams(vmem_limit_bytes=24 << 20),
             name="adjoint",
-        )(predicted, residual, blocks, spectra, bas_h, bas_l, tra_h, tra_l)
+        )(predicted, residual, blocks, spectra, *map(in_hbm, (bas_h, bas_l, tra_h, tra_l)))
 
     in_specs = (P(None, "gx", "gy"), P("gx", "gy"), P("gx", "gy"), P())
     out_specs = (P("gx", "gy"), P("gx", "gy"), P(None, "gx", "gy"))

time: 57.7 us -> 48.8 us (0.85)
  the two profiles are of different devices: /device:TPU:60 before, /device:TPU:164 now
where the time goes in v1:
time: 48.8 us; the launch traced here: 48.7 us
  Pallas kernels  48.1 us (99%)
  between operations  0.64 us (1%)
    pallas_call x1, Pallas kernels, body(): pl.pallas_call(functools.partial(forward_kernel, counts), out_shape=(pltp...  43.9 us
    pallas_call x1, Pallas kernels, body(): pl.pallas_call(adjoint_kernel, out_shape=(jax.ShapeDtypeStruct((tile, til...  4.14 us

profile of v1, /device:TPU:164, one launch (start us, length us, event | category | flops | bytes accessed | tf_op | source)
XLA Modules:
  0.0 48.7 jit_solution(9620805907083897303)
XLA Ops:
  0.6 43.9 %forward.1 = (f32[256,256]{1,0:T(8,128)S(1)}, f32[256,256]{1,0:T(8,128)S(1)}, f32[512,512]{1,0:T(8,128)S(1)}, f32[2,256,256]{2,1,0:T(8,128)S(1)}) custom-call(s32[2]{0:T(128)} %layer_index.1, f32[2,256,256]{2,1,0:T(8,128)} %density.1, f32[256,256]{1,0:T(8,128)} %observed.1, s32[256,256]{1,0:T(8,128)} %stations.1, bf16[512,512]{1,0:T(8,128)(2,1)} %constant.12.clone.bas_h, ...), custom_call_target="tpu_custom_call" | custom-call | tf_op jit(solution)/shard_map/forward/pallas_call | solution.py:314
  44.6 4.1 %adjoint.1 = (f32[256,256]{1,0:T(8,128)}, f32[256,256]{1,0:T(8,128)}, f32[2,256,256]{2,1,0:T(8,128)}) custom-call(f32[256,256]{1,0:T(8,128)S(1)} %get-tuple-element.7.predicted, f32[256,256]{1,0:T(8,128)S(1)} %get-tuple-element.8.residual, f32[512,512]{1,0:T(8,128)S(1)} %get-tuple-element.9.blocks, f32[2,256,256]{2,1,0:T(8,128)S(1)} %get-tuple-element.10.spectra, ...), custom_call_target="tpu_custom_call" | custom-call | tf_op jit(solution)/shard_map/adjoint/pallas_call | solution.py:344

commit v2 on v1

v2 whole, which is shorter than its diff:
```python
import functools
import math

import jax
import jax.numpy as jnp
import numpy as np
from jax import lax
from jax.experimental import pallas as pl
from jax.experimental.pallas import tpu as pltpu
from jax.sharding import PartitionSpec as P

RADIUS = 128
LAYERS_ALL = 512
MESH = pl.DeviceIdType.MESH
F32 = jnp.float32
BF16 = jnp.bfloat16

DIRS = ((1, 0), (-1, 0), (0, 1), (0, -1))


def halves(table):
    high = table.astype(BF16)
    return high, (table - high.astype(np.float64)).astype(BF16)


def tables(length):
    half = length // 2
    odd = 2 * np.arange(half)[:, None] + 1
    phase = (odd * (2 * np.arange(length)[None, :] - length + 1)) % (4 * length)
    angle = phase * (2.0 * math.pi / (4 * length))
    basis = np.concatenate([np.cos(angle), np.sin(angle)])
    ends = np.split(basis, (RADIUS, length - RADIUS), axis=1)
    basis = np.concatenate([ends[0], ends[2], ends[1]], axis=1)
    ticks = np.arange(half)[None, :]
    kphase = (odd * ticks) % (2 * length)
    weight = np.where(ticks == 0, 1.0, 2.0) * (ticks <= RADIUS) / half
    cosines = np.cos(kphase * (2.0 * math.pi / (2 * length))) * weight
    return halves(basis), halves(np.ascontiguousarray(basis.T)), halves(cosines)


def dot(left, right):
    return lax.dot_general(left, right, (((1,), (0,)), ((), ())), preferred_element_type=F32)


def dot_t(left, right):
    return lax.dot_general(left, right, (((1,), (1,)), ((), ())), preferred_element_type=F32)


def in_hbm(array):
    return pltpu.with_memory_space_constraint(array, pltpu.HBM)


def split(value):
    high = value.astype(BF16)
    return high, (value - high.astype(F32)).astype(BF16)


def product(left, right, how=dot):
    return how(left[0], right[0]) + (how(left[1], right[0]) + how(left[0], right[1]))


def part(refs, rows, cols):
    return refs[0][rows, cols], refs[1][rows, cols]


def put(refs, rows, cols, value):
    refs[0][rows, cols], refs[1][rows, cols] = split(value)


def forward_kernel(
    counts,
    layer_index, density, observed, stations, bas_h, bas_l, tra_h, tra_l, cos_h, cos_l,
    predicted, residual, blocks, spectra, b_h, b_l, t_h, t_l,
    den, obs, sta, c_h, c_l,
    s_h, s_l, z_h, z_l, total, big, win, wait_x, from_x, from_y, from_c,
    index, index_sem, load_sem, send_sem, recv_sem,
):
    gx, gy = lax.axis_index("gx"), lax.axis_index("gy")
    nx, ny = counts
    layers, tile = den.shape[0], den.shape[1]
    length = tile + 2 * RADIUS
    half = length // 2
    low, high, mid = slice(0, RADIUS), slice(RADIUS, 2 * RADIUS), slice(2 * RADIUS, length)
    edge, every = slice(0, 2 * RADIUS), slice(0, length)
    first, last = slice(2 * RADIUS, 3 * RADIUS), slice(length - RADIUS, length)
    own = slice(0, tile)

    def there(dx, dy):
        if dx:
            return gx < nx - 1 if dx > 0 else gx > 0
        return gy < ny - 1 if dy > 0 else gy > 0

    def target(dx, dy):
        return {"gx": gx + dx, "gy": gy + dy}

    barrier = pltpu.get_barrier_semaphore()
    for dx, dy in DIRS:
        @pl.when(there(dx, dy))
        def _(dx=dx, dy=dy):
            pl.semaphore_signal(barrier, inc=1, device_id=target(dx, dy), device_id_type=MESH)

    pairs = ((cos_h, c_h), (cos_l, c_l), (density, den), (tra_h, t_h), (tra_l, t_l), (bas_h, b_h), (bas_l, b_l), (observed, obs), (stations, sta))
    loads = [pltpu.make_async_copy(src, dst, load_sem.at[i]) for i, (src, dst) in enumerate(pairs)]
    index_load = pltpu.make_async_copy(layer_index, index, index_sem)
    index_load.start()
    for load in loads:
        load.start()

    @pl.when(gx == 0)
    def _():
        win[low, mid] = jnp.zeros((RADIUS, tile), F32)

    @pl.when(gx == nx - 1)
    def _():
        win[high, mid] = jnp.zeros((RADIUS, tile), F32)

    @pl.when(gy == 0)
    def _():
        win[:, low] = jnp.zeros((length, RADIUS), F32)

    @pl.when(gy == ny - 1)
    def _():
        win[:, high] = jnp.zeros((length, RADIUS), F32)

    rows = lax.broadcasted_iota(jnp.int32, (half, half), 0).astype(F32)
    cols = lax.broadcasted_iota(jnp.int32, (half, half), 1).astype(F32)
    flat = rows * rows + cols * cols
    index_load.wait()
    loads[0].wait()
    loads[1].wait()
    cosines = (c_h[...], c_l[...])
    for layer in range(layers):
        depth = RADIUS * (0.375 + index[layer].astype(F32) / LAYERS_ALL)
        square = flat + depth * depth
        inverse = lax.rsqrt(square)
        value = (depth * depth) * (inverse * inverse * inverse)
        left = product(cosines, split(value))
        spectra[layer] = product(split(left), cosines, dot_t)

    for load in loads[2:7]:
        load.wait()
    basis, trans, work, mixed = (b_h, b_l), (t_h, t_l), (s_h, s_l), (z_h, z_l)
    bands = [slice(r * half, (r + 1) * half) for r in range(2)]
    for layer in range(layers):
        put(work, own, every, product(split(den[layer]), part(trans, mid, every)))
        spectrum = spectra[layer]
        for band in bands:
            out = product(part(basis, band, mid), part(work, own, every))
            for at in bands:
                term = spectrum * out[:, at]
                if layer == 0:
                    total[band, at] = term
                elif layer < layers - 1:
                    total[band, at] = total[band, at] + term
                else:
                    put(mixed, band, at, total[band, at] + term)

    def remote(kind, k, src, dst):
        return pltpu.make_async_remote_copy(
            src_ref=src, dst_ref=dst, send_sem=send_sem.at[kind, k], recv_sem=recv_sem.at[kind, k],
            device_id=target(*DIRS[k]), device_id_type=MESH,
        )

    beyond = {1: high, -1: low}
    near = {1: last, -1: first}
    far = {1: low, -1: high}

    def fold_corner(k):
        return remote(0, k, big.at[edge, beyond[DIRS[k][1]]], from_c.at[k - 2])

    def fold_y(k):
        return remote(1, k, big.at[mid, beyond[DIRS[k][1]]], from_y.at[k - 2])

    def fold_x(k):
        return remote(1, k, big.at[beyond[DIRS[k][0]], mid], from_x.at[k])

    def halo_x(k):
        side = DIRS[k][0]
        return remote(2, k, win.at[near[side], mid], win.at[far[side], mid])

    def halo_y(k):
        side = DIRS[k][1]
        return remote(2, k, win.at[mid, near[side]], win.at[mid, far[side]])

    def halo_corner(k):
        side = DIRS[k][1]
        return remote(3, k, win.at[edge, near[side]], win.at[edge, far[side]])

    along_x, along_y = (0, 1), (2, 3)

    def start(make, ks):
        for k in ks:
            @pl.when(there(*DIRS[k]))
            def _(k=k):
                make(k).start()

    def sent(make, ks):
        for k in ks:
            @pl.when(there(*DIRS[k]))
            def _(k=k):
                make(k).wait_send()

    def received(make, ks, then=None):
        for k in ks:
            dx, dy = DIRS[k]
            @pl.when(there(-dx, -dy))
            def _(k=k):
                make(k).wait_recv()
                if then is not None:
                    then(k)

    def mix(cs):
        for band in bands:
            put(work, band, cs, product(part(mixed, band, every), part(basis, every, cs)))

    def back(rs, cs):
        big[rs, cs] = product(part(trans, rs, every), part(work, every, cs))

    mix(edge)
    back(edge, edge)
    sides_x = 2 - (gx == 0).astype(jnp.int32) - (gx == nx - 1).astype(jnp.int32)
    sides_y = 2 - (gy == 0).astype(jnp.int32) - (gy == ny - 1).astype(jnp.int32)
    pl.semaphore_wait(barrier, sides_x + sides_y)
    start(fold_corner, along_y)
    mix(mid)
    back(edge, mid)

    def add_corner(k):
        cs = {1: first, -1: last}[DIRS[k][1]]
        big[edge, cs] = big[edge, cs] + from_c[k - 2]

    received(fold_corner, along_y, add_corner)
    start(fold_x, along_x)
    back(mid, edge)
    start(fold_y, along_y)
    back(mid, mid)
    for load in loads[7:]:
        load.wait()

    def add_y(k):
        cs = {1: first, -1: last}[DIRS[k][1]]
        big[mid, cs] = big[mid, cs] + from_y[k - 2]

    def add_x(k):
        rs = {1: first, -1: last}[DIRS[k][0]]
        big[rs, mid] = big[rs, mid] + from_x[k]

    received(fold_y, along_y, add_y)
    received(fold_x, along_x, add_x)
    total_pred = big[mid, mid]
    misfit = sta[...].astype(F32) * (total_pred - obs[...])
    win[mid, mid] = misfit
    start(halo_x, along_x)
    start(halo_y, along_y)
    predicted[...] = total_pred
    residual[...] = misfit

    received(halo_y, along_y)
    put(work, mid, every, product(split(win[mid, :]), part(trans, every, every)))
    for band in bands:
        total[band, :] = product(part(basis, band, mid), part(work, mid, every))

    received(halo_x, along_x)
    start(halo_corner, along_y)
    wait_x[...] = product(split(win[edge, mid]), part(trans, mid, every))
    received(halo_corner, along_y)
    put(work, edge, every, wait_x[...] + product(split(win[edge, edge]), part(trans, edge, every)))
    for band in bands:
        blocks[band, :] = total[band, :] + product(part(basis, band, edge), part(work, edge, every))
    sent(fold_corner, along_y)
    sent(fold_y, along_y)
    sent(fold_x, along_x)
    sent(halo_x, along_x)
    sent(halo_y, along_y)
    sent(halo_corner, along_y)


def adjoint_kernel(
    predicted, residual, blocks, spectra, b_h, b_l, t_h, t_l,
    predicted_out, residual_out, gradient,
    z_h, z_l, w_h, w_l, grad, out_sem,
):
    layers, tile = spectra.shape[0], residual.shape[0]
    length = tile + 2 * RADIUS
    half = length // 2
    mid, every, own = slice(2 * RADIUS, length), slice(0, length), slice(0, tile)
    bands = [slice(r * half, (r + 1) * half) for r in range(2)]
    basis, trans, mixed, work = (b_h, b_l), (t_h, t_l), (z_h, z_l), (w_h, w_l)
    stores = [
        pltpu.make_async_copy(predicted, predicted_out, out_sem.at[0]),
        pltpu.make_async_copy(residual, residual_out, out_sem.at[1]),
    ]
    for store in stores:
        store.start()
    for layer in range(layers):
        spectrum = spectra[layer]
        for band in bands:
            for at in bands:
                put(mixed, band, at, spectrum * blocks[band, at])
        for band in bands:
            put(work, band, own, product(part(mixed, band, every), part(basis, every, mid)))
        grad[layer] = product(part(trans, mid, every), part(work, every, own))
        store = pltpu.make_async_copy(grad.at[layer], gradient.at[layer], out_sem.at[2 + layer])
        store.start()
        stores.append(store)
    for store in stores:
        store.wait()


def solution(mesh):
    counts = (mesh.shape["gx"], mesh.shape["gy"])

    def body(density, observed, stations, layer_index):
        layers, tile = density.shape[0], density.shape[1]
        length = tile + 2 * RADIUS
        half = length // 2
        (bas_h, bas_l), (tra_h, tra_l), (cos_h, cos_l) = tables(length)
        anywhere = pl.BlockSpec(memory_space=pl.ANY)
        vmem = pl.BlockSpec(memory_space=pltpu.VMEM)
        big = pltpu.VMEM((length, length), F32)
        wide = pltpu.VMEM((length, length), BF16)
        small = pltpu.VMEM((half, half), BF16)
        predicted, residual, blocks, spectra, *kept = pl.pallas_call(
            functools.partial(forward_kernel, counts),
            out_shape=(
                pltpu.VMEM((tile, tile), F32),
                pltpu.VMEM((tile, tile), F32),
                pltpu.VMEM((length, length), F32),
                pltpu.VMEM((layers, half, half), F32),
                wide, wide, wide, wide,
            ),
            in_specs=[anywhere] * 10,
            out_specs=(vmem,) * 8,
            scratch_shapes=[
                pltpu.VMEM(density.shape, F32),
                pltpu.VMEM((tile, tile), F32),
                pltpu.VMEM((tile, tile), jnp.int32),
                small, small,
                wide, wide, wide, wide, big, big, big,
                pltpu.VMEM((2 * RADIUS, length), F32),
                pltpu.VMEM((2, RADIUS, tile), F32),
                pltpu.VMEM((2, tile, RADIUS), F32),
                pltpu.VMEM((2, 2 * RADIUS, RADIUS), F32),
                pltpu.SMEM((layers,), jnp.int32),
                pltpu.SemaphoreType.DMA,
                pltpu.SemaphoreType.DMA((9,)),
                pltpu.SemaphoreType.DMA((4, 4)),
                pltpu.SemaphoreType.DMA((4, 4)),
            ],
            compiler_params=pltpu.CompilerParams(
                collective_id=0, has_side_effects=True, vmem_limit_bytes=32 << 20
            ),
            name="forward",
        )(*map(in_hbm, (layer_index, density, observed, stations, bas_h, bas_l, tra_h, tra_l, cos_h, cos_l)))
        return pl.pallas_call(
            adjoint_kernel,
            out_shape=(
                jax.ShapeDtypeStruct((tile, tile), F32),
                jax.ShapeDtypeStruct((tile, tile), F32),
                jax.ShapeDtypeStruct((layers, tile, tile), F32),
            ),
            in_specs=[vmem] * 8,
            out_specs=(anywhere,) * 3,
            scratch_shapes=[
                wide, wide,
                pltpu.VMEM((length, tile), BF16),
                pltpu.VMEM((length, tile), BF16),
                pltpu.VMEM((layers, tile, tile), F32),
                pltpu.SemaphoreType.DMA((2 + layers,)),
            ],
            compiler_params=pltpu.CompilerParams(vmem_limit_bytes=24 << 20),
            name="adjoint",
        )(predicted, residual, blocks, spectra, *kept)

    in_specs = (P(None, "gx", "gy"), P("gx", "gy"), P("gx", "gy"), P())
    out_specs = (P("gx", "gy"), P("gx", "gy"), P(None, "gx", "gy"))
    return jax.shard_map(body, mesh=mesh, in_specs=in_specs, out_specs=out_specs, check_vma=False)
```

time: 48.8 us -> 41.1 us (0.84)
  the two profiles are of different devices: /device:TPU:164 before, /device:TPU:29 now
where the time goes in v2:
time: 41.1 us
  Pallas kernels  40.4 us (98%)
  between operations  0.64 us (2%)
    pallas_call x1, Pallas kernels, body(): pl.pallas_call(functools.partial(forward_kernel, counts), out_shape=(pltp...  37.7 us
    pallas_call x1, Pallas kernels, body(): pl.pallas_call(adjoint_kernel, out_shape=(jax.ShapeDtypeStruct((tile, til...  2.73 us

profile of v2, /device:TPU:29, one launch (start us, length us, event | category | flops | bytes accessed | tf_op | source)
XLA Modules:
  0.0 41.1 jit_solution(7803357536340342314)
XLA Ops:
  0.6 37.7 %forward.1 = (f32[256,256]{1,0:T(8,128)S(1)}, f32[256,256]{1,0:T(8,128)S(1)}, f32[512,512]{1,0:T(8,128)S(1)}, f32[2,256,256]{2,1,0:T(8,128)S(1)}, bf16[512,512]{...) custom-call(s32[2]{0:T(128)} %layer_index.1, ...), custom_call_target="tpu_custom_call" | custom-call | tf_op jit(solution)/shard_map/forward/pallas_call | solution.py:323
  38.3 2.7 %adjoint.1 = (f32[256,256]{1,0:T(8,128)}, f32[256,256]{1,0:T(8,128)}, f32[2,256,256]{2,1,0:T(8,128)}) custom-call(f32[256,256]{1,0:T(8,128)S(1)} %get-tuple-element.11.predicted, f32[256,256]{1,0:T(8,128)S(1)} %get-tuple-element.12.residual, f32[512,512]{1,0:T(8,128)S(1)} %get-tuple-element.13.blocks, f32[2,256,256]{2,1,0:T(8,128)S(1)} %get-tuple-element.14.spectra, ...), custom_call_target="tpu_custom_call" | custom-call | tf_op jit(solution)/shard_map/adjoint/pallas_call | solution.py:355

commit v3 on v2

--- a/solution.py
+++ b/solution.py
@@ -15,7 +15,7 @@
 F32 = jnp.float32
 BF16 = jnp.bfloat16
 
-DIRS = ((1, 0), (-1, 0), (0, 1), (0, -1))
+CHUNKS = 2
 
 
 def halves(table):
@@ -72,7 +72,7 @@
     layer_index, density, observed, stations, bas_h, bas_l, tra_h, tra_l, cos_h, cos_l,
     predicted, residual, blocks, spectra, b_h, b_l, t_h, t_l,
     den, obs, sta, c_h, c_l,
-    s_h, s_l, z_h, z_l, total, big, win, wait_x, from_x, from_y, from_c,
+    s_h, s_l, z_h, z_l, total, big, win, wait_x, from_x, from_y, from_c, from_d,
     index, index_sem, load_sem, send_sem, recv_sem,
 ):
     gx, gy = lax.axis_index("gx"), lax.axis_index("gy")
@@ -85,19 +85,34 @@
     first, last = slice(2 * RADIUS, 3 * RADIUS), slice(length - RADIUS, length)
     own = slice(0, tile)
 
-    def there(dx, dy):
-        if dx:
-            return gx < nx - 1 if dx > 0 else gx > 0
-        return gy < ny - 1 if dy > 0 else gy > 0
-
-    def target(dx, dy):
-        return {"gx": gx + dx, "gy": gy + dy}
+    even = lax.rem(gy, 2) == 0
+    partner = gy + jnp.where(even, 1, -1)
+    outer = gy + jnp.where(even, -1, 1)
+    has_outer = (outer >= 0) & (outer < ny)
+    steps = (1, -1)
+
+    def columns(for_even, for_odd):
+        return pl.ds(pl.multiple_of(jnp.where(even, for_even, for_odd), RADIUS), RADIUS)
+
+    core_edge, far_edge = columns(RADIUS, 0), columns(0, RADIUS)
+    core_near, far_near = columns(length - RADIUS, 2 * RADIUS), columns(2 * RADIUS, length - RADIUS)
+
+    def there(dx):
+        return gx < nx - 1 if dx > 0 else gx > 0
+
+    def only_if(condition, act):
+        pl.when(condition)(act)
 
     barrier = pltpu.get_barrier_semaphore()
-    for dx, dy in DIRS:
-        @pl.when(there(dx, dy))
-        def _(dx=dx, dy=dy):
-            pl.semaphore_signal(barrier, inc=1, device_id=target(dx, dy), device_id_type=MESH)
+
+    def greet(x, y):
+        pl.semaphore_signal(barrier, inc=1, device_id={"gx": x, "gy": y}, device_id_type=MESH)
+
+    greet(gx, partner)
+    only_if(has_outer, lambda: greet(gx, outer))
+    for dx in steps:
+        only_if(there(dx), lambda: greet(gx + dx, gy))
+        only_if(there(dx) & has_outer, lambda: greet(gx + dx, outer))
 
     pairs = ((cos_h, c_h), (cos_l, c_l), (density, den), (tra_h, t_h), (tra_l, t_l), (bas_h, b_h), (bas_l, b_l), (observed, obs), (stations, sta))
     loads = [pltpu.make_async_copy(src, dst, load_sem.at[i]) for i, (src, dst) in enumerate(pairs)]
@@ -108,11 +123,11 @@
 
     @pl.when(gx == 0)
     def _():
-        win[low, mid] = jnp.zeros((RADIUS, tile), F32)
+        win[low, :] = jnp.zeros((RADIUS, length), F32)
 
     @pl.when(gx == nx - 1)
     def _():
-        win[high, mid] = jnp.zeros((RADIUS, tile), F32)
+        win[high, :] = jnp.zeros((RADIUS, length), F32)
 
     @pl.when(gy == 0)
     def _():
@@ -155,59 +170,57 @@
                 else:
                     put(mixed, band, at, total[band, at] + term)
 
-    def remote(kind, k, src, dst):
+    def remote(number, src, dst, x, y):
         return pltpu.make_async_remote_copy(
-            src_ref=src, dst_ref=dst, send_sem=send_sem.at[kind, k], recv_sem=recv_sem.at[kind, k],
-            device_id=target(*DIRS[k]), device_id_type=MESH,
+            src_ref=src, dst_ref=dst, send_sem=send_sem.at[number], recv_sem=recv_sem.at[number],
+            device_id={"gx": x, "gy": y}, device_id_type=MESH,
         )
+
+    depth_of = RADIUS // CHUNKS
+
+    def piece(rs, c):
+        return slice(rs.start + c * depth_of, rs.start + (c + 1) * depth_of)
 
     beyond = {1: high, -1: low}
     near = {1: last, -1: first}
     far = {1: low, -1: high}
-
-    def fold_corner(k):
-        return remote(0, k, big.at[edge, beyond[DIRS[k][1]]], from_c.at[k - 2])
-
-    def fold_y(k):
-        return remote(1, k, big.at[mid, beyond[DIRS[k][1]]], from_y.at[k - 2])
-
-    def fold_x(k):
-        return remote(1, k, big.at[beyond[DIRS[k][0]], mid], from_x.at[k])
-
-    def halo_x(k):
-        side = DIRS[k][0]
-        return remote(2, k, win.at[near[side], mid], win.at[far[side], mid])
-
-    def halo_y(k):
-        side = DIRS[k][1]
-        return remote(2, k, win.at[mid, near[side]], win.at[mid, far[side]])
-
-    def halo_corner(k):
-        side = DIRS[k][1]
-        return remote(3, k, win.at[edge, near[side]], win.at[edge, far[side]])
-
-    along_x, along_y = (0, 1), (2, 3)
-
-    def start(make, ks):
-        for k in ks:
-            @pl.when(there(*DIRS[k]))
-            def _(k=k):
-                make(k).start()
-
-    def sent(make, ks):
-        for k in ks:
-            @pl.when(there(*DIRS[k]))
-            def _(k=k):
-                make(k).wait_send()
-
-    def received(make, ks, then=None):
-        for k in ks:
-            dx, dy = DIRS[k]
-            @pl.when(there(-dx, -dy))
-            def _(k=k):
-                make(k).wait_recv()
-                if then is not None:
-                    then(k)
+    lands = {1: first, -1: last}
+    each = [(c, dx) for c in range(CHUNKS) for dx in steps]
+
+    def numbered(kind, c, dx):
+        return 5 + (kind * CHUNKS + c) * 2 + (dx < 0)
+
+    def fold_core():
+        return remote(0, big.at[edge, core_edge], from_c, gx, partner)
+
+    def fold_partner():
+        return remote(1, big.at[mid, core_edge], from_y.at[0], gx, partner)
+
+    def fold_outer():
+        return remote(2, big.at[mid, far_edge], from_y.at[1], gx, outer)
+
+    def fold_x(c, dx):
+        rs = slice(c * depth_of, (c + 1) * depth_of)
+        return remote(numbered(0, c, dx), big.at[piece(beyond[dx], c), mid], from_x.at[int(dx < 0), rs], gx + dx, gy)
+
+    def fold_d(c, dx):
+        rs = slice(c * depth_of, (c + 1) * depth_of)
+        return remote(numbered(1, c, dx), big.at[piece(beyond[dx], c), far_edge], from_d.at[int(dx < 0), rs], gx + dx, outer)
+
+    def halo_partner():
+        return remote(3, win.at[mid, core_near], win.at[mid, far_edge], gx, partner)
+
+    def halo_outer():
+        return remote(4, win.at[mid, far_near], win.at[mid, core_edge], gx, outer)
+
+    def halo_x(c, dx):
+        return remote(numbered(2, c, dx), win.at[piece(near[dx], c), mid], win.at[piece(far[dx], c), mid], gx + dx, gy)
+
+    def halo_d(c, dx):
+        return remote(numbered(3, c, dx), win.at[piece(near[dx], c), far_near], win.at[piece(far[dx], c), core_edge], gx + dx, outer)
+
+    def halo_core(c, dx):
+        return remote(numbered(4, c, dx), win.at[piece(far[dx], c), core_near], win.at[piece(far[dx], c), far_edge], gx, partner)
 
     def mix(cs):
         for band in bands:
@@ -218,61 +231,98 @@
 
     mix(edge)
     back(edge, edge)
-    sides_x = 2 - (gx == 0).astype(jnp.int32) - (gx == nx - 1).astype(jnp.int32)
-    sides_y = 2 - (gy == 0).astype(jnp.int32) - (gy == ny - 1).astype(jnp.int32)
-    pl.semaphore_wait(barrier, sides_x + sides_y)
-    start(fold_corner, along_y)
+    sides = 2 - (gx == 0).astype(jnp.int32) - (gx == nx - 1).astype(jnp.int32)
+    pl.semaphore_wait(barrier, (sides + 1) * jnp.where(has_outer, 2, 1))
+    fold_core().start()
+    for c, dx in each:
+        only_if(there(dx) & has_outer, lambda: fold_d(c, dx).start())
     mix(mid)
     back(edge, mid)
-
-    def add_corner(k):
-        cs = {1: first, -1: last}[DIRS[k][1]]
-        big[edge, cs] = big[edge, cs] + from_c[k - 2]
-
-    received(fold_corner, along_y, add_corner)
-    start(fold_x, along_x)
+    fold_core().wait_recv()
+    big[edge, core_near] = big[edge, core_near] + from_c[...]
+    for c, dx in each:
+        only_if(there(dx), lambda: fold_x(c, dx).start())
     back(mid, edge)
-    start(fold_y, along_y)
+    fold_partner().start()
+    only_if(has_outer, lambda: fold_outer().start())
     back(mid, mid)
     for load in loads[7:]:
         load.wait()
 
-    def add_y(k):
-        cs = {1: first, -1: last}[DIRS[k][1]]
-        big[mid, cs] = big[mid, cs] + from_y[k - 2]
-
-    def add_x(k):
-        rs = {1: first, -1: last}[DIRS[k][0]]
-        big[rs, mid] = big[rs, mid] + from_x[k]
-
-    received(fold_y, along_y, add_y)
-    received(fold_x, along_x, add_x)
-    total_pred = big[mid, mid]
-    misfit = sta[...].astype(F32) * (total_pred - obs[...])
-    win[mid, mid] = misfit
-    start(halo_x, along_x)
-    start(halo_y, along_y)
-    predicted[...] = total_pred
-    residual[...] = misfit
-
-    received(halo_y, along_y)
+    fold_partner().wait_recv()
+    big[mid, core_near] = big[mid, core_near] + from_y[0]
+
+    @pl.when(has_outer)
+    def _():
+        fold_outer().wait_recv()
+        big[mid, far_near] = big[mid, far_near] + from_y[1]
+
+    for c, dx in each:
+        rs = piece(lands[dx], c)
+        tile_rows = slice(rs.start - 2 * RADIUS, rs.stop - 2 * RADIUS)
+        at = slice(c * depth_of, (c + 1) * depth_of)
+
+        @pl.when(there(-dx))
+        def _():
+            fold_x(c, dx).wait_recv()
+            big[rs, mid] = big[rs, mid] + from_x[int(dx < 0), at]
+
+        @pl.when(there(-dx) & has_outer)
+        def _():
+            fold_d(c, dx).wait_recv()
+            big[rs, far_near] = big[rs, far_near] + from_d[int(dx < 0), at]
+
+        ahead = big[rs, mid]
+        win[rs, mid] = sta[tile_rows, :].astype(F32) * (ahead - obs[tile_rows, :])
+        only_if(there(-dx), lambda: halo_x(c, -dx).start())
+        only_if(there(-dx) & has_outer, lambda: halo_d(c, -dx).start())
+
+    halo_partner().start()
+    only_if(has_outer, lambda: halo_outer().start())
+    predicted[...] = big[mid, mid]
+    residual[...] = win[mid, mid]
+
+    halo_partner().wait_recv()
+    only_if(has_outer, lambda: halo_outer().wait_recv())
     put(work, mid, every, product(split(win[mid, :]), part(trans, every, every)))
     for band in bands:
         total[band, :] = product(part(basis, band, mid), part(work, mid, every))
 
-    received(halo_x, along_x)
-    start(halo_corner, along_y)
+    for c, dx in each:
+        @pl.when(there(-dx))
+        def _():
+            halo_x(c, dx).wait_recv()
+            halo_core(c, dx).start()
+
     wait_x[...] = product(split(win[edge, mid]), part(trans, mid, every))
-    received(halo_corner, along_y)
+    for c, dx in each:
+        only_if(there(-dx), lambda: halo_core(c, dx).wait_recv())
+        only_if(there(-dx) & has_outer, lambda: halo_d(c, dx).wait_recv())
     put(work, edge, every, wait_x[...] + product(split(win[edge, edge]), part(trans, edge, every)))
     for band in bands:
         blocks[band, :] = total[band, :] + product(part(basis, band, edge), part(work, edge, every))
-    sent(fold_corner, along_y)
-    sent(fold_y, along_y)
-    sent(fold_x, along_x)
-    sent(halo_x, along_x)
-    sent(halo_y, along_y)
-    sent(halo_corner, along_y)
+
+    fold_core().wait_send()
+    fold_partner().wait_send()
+    halo_partner().wait_send()
+
+    @pl.when(has_outer)
+    def _():
+        fold_outer().wait_send()
+        halo_outer().wait_send()
+
+    for c, dx in each:
+        @pl.when(there(dx))
+        def _():
+            fold_x(c, dx).wait_send()
+            halo_x(c, dx).wait_send()
+
+        @pl.when(there(dx) & has_outer)
+        def _():
+            fold_d(c, dx).wait_send()
+            halo_d(c, dx).wait_send()
+
+        only_if(there(-dx), lambda: halo_core(c, dx).wait_send())
 
 
 def adjoint_kernel(
@@ -340,12 +390,13 @@
                 pltpu.VMEM((2 * RADIUS, length), F32),
                 pltpu.VMEM((2, RADIUS, tile), F32),
                 pltpu.VMEM((2, tile, RADIUS), F32),
-                pltpu.VMEM((2, 2 * RADIUS, RADIUS), F32),
+                pltpu.VMEM((2 * RADIUS, RADIUS), F32),
+                pltpu.VMEM((2, RADIUS, RADIUS), F32),
                 pltpu.SMEM((layers,), jnp.int32),
                 pltpu.SemaphoreType.DMA,
                 pltpu.SemaphoreType.DMA((9,)),
-                pltpu.SemaphoreType.DMA((4, 4)),
-                pltpu.SemaphoreType.DMA((4, 4)),
+                pltpu.SemaphoreType.DMA((5 + 10 * CHUNKS,)),
+                pltpu.SemaphoreType.DMA((5 + 10 * CHUNKS,)),
             ],
             compiler_params=pltpu.CompilerParams(
                 collective_id=0, has_side_effects=True, vmem_limit_bytes=32 << 20

time: 41.1 us -> 38.7 us (0.942)
  the two profiles are of different devices: /device:TPU:29 before, /device:TPU:57 now
where the time goes in v3:
time: 38.7 us
  Pallas kernels  38 us (98%)
  between operations  0.64 us (2%)
    pallas_call x1, Pallas kernels, body(): pl.pallas_call(functools.partial(forward_kernel, counts), out_shape=(pltp...  35.3 us
    pallas_call x1, Pallas kernels, body(): pl.pallas_call(adjoint_kernel, out_shape=(jax.ShapeDtypeStruct((tile, til...  2.73 us

profile of v3, /device:TPU:57, one launch (start us, length us, event | category | flops | bytes accessed | tf_op | source)
XLA Modules:
  0.0 38.7 jit_solution(7703542112680540583)
XLA Ops:
  0.6 35.3 %forward.1 = (f32[256,256]{1,0:T(8,128)S(1)}, f32[256,256]{1,0:T(8,128)S(1)}, f32[512,512]{1,0:T(8,128)S(1)}, f32[2,256,256]{2,1,0:T(8,128)S(1)}, bf16[512,512]{...) custom-call(s32[2]{0:T(128)} %layer_index.1, ...), custom_call_target="tpu_custom_call" | custom-call | tf_op jit(solution)/shard_map/forward/pallas_call | solution.py:373
  35.9 2.7 %adjoint.1 = (f32[256,256]{1,0:T(8,128)}, f32[256,256]{1,0:T(8,128)}, f32[2,256,256]{2,1,0:T(8,128)}) custom-call(f32[256,256]{1,0:T(8,128)S(1)} %get-tuple-element.11.predicted, f32[256,256]{1,0:T(8,128)S(1)} %get-tuple-element.12.residual, f32[512,512]{1,0:T(8,128)S(1)} %get-tuple-element.13.blocks, f32[2,256,256]{2,1,0:T(8,128)S(1)} %get-tuple-element.14.spectra, ...), custom_call_target="tpu_custom_call" | custom-call | tf_op jit(solution)/shard_map/adjoint/pallas_call | solution.py:406

commit v4 on v3

--- a/solution.py
+++ b/solution.py
@@ -15,7 +15,7 @@
 F32 = jnp.float32
 BF16 = jnp.bfloat16
 
-CHUNKS = 2
+CHUNKS = 1
 
 
 def halves(table):
@@ -83,7 +83,6 @@
     low, high, mid = slice(0, RADIUS), slice(RADIUS, 2 * RADIUS), slice(2 * RADIUS, length)
     edge, every = slice(0, 2 * RADIUS), slice(0, length)
     first, last = slice(2 * RADIUS, 3 * RADIUS), slice(length - RADIUS, length)
-    own = slice(0, tile)
 
     even = lax.rem(gy, 2) == 0
     partner = gy + jnp.where(even, 1, -1)
@@ -114,11 +113,16 @@
         only_if(there(dx), lambda: greet(gx + dx, gy))
         only_if(there(dx) & has_outer, lambda: greet(gx + dx, outer))
 
-    pairs = ((cos_h, c_h), (cos_l, c_l), (density, den), (tra_h, t_h), (tra_l, t_l), (bas_h, b_h), (bas_l, b_l), (observed, obs), (stations, sta))
+    pairs = [(cos_h, c_h), (cos_l, c_l)]
+    pairs += [(density.at[layer], den.at[layer]) for layer in range(layers)]
+    pairs += [(tra_h.at[mid], t_h.at[mid]), (tra_l.at[mid], t_l.at[mid])]
+    pairs += [(bas_h.at[:, mid], b_h.at[:, mid]), (bas_l.at[:, mid], b_l.at[:, mid])]
+    pairs += [(bas_h.at[:, edge], b_h.at[:, edge]), (bas_l.at[:, edge], b_l.at[:, edge])]
+    pairs += [(tra_h.at[edge], t_h.at[edge]), (tra_l.at[edge], t_l.at[edge]), (observed, obs), (stations, sta)]
     loads = [pltpu.make_async_copy(src, dst, load_sem.at[i]) for i, (src, dst) in enumerate(pairs)]
     index_load = pltpu.make_async_copy(layer_index, index, index_sem)
     index_load.start()
-    for load in loads:
+    for load in loads[: layers + 6]:
         load.start()
 
     @pl.when(gx == 0)
@@ -152,11 +156,14 @@
         left = product(cosines, split(value))
         spectra[layer] = product(split(left), cosines, dot_t)
 
-    for load in loads[2:7]:
+    for load in loads[2 : layers + 6]:
         load.wait()
+    for load in loads[layers + 6 :]:
+        load.start()
     basis, trans, work, mixed = (b_h, b_l), (t_h, t_l), (s_h, s_l), (z_h, z_l)
     bands = [slice(r * half, (r + 1) * half) for r in range(2)]
     for layer in range(layers):
+        own = slice(layer % 2 * tile, (layer % 2 + 1) * tile)
         put(work, own, every, product(split(den[layer]), part(trans, mid, every)))
         spectrum = spectra[layer]
         for band in bands:
@@ -188,7 +195,7 @@
     each = [(c, dx) for c in range(CHUNKS) for dx in steps]
 
     def numbered(kind, c, dx):
-        return 5 + (kind * CHUNKS + c) * 2 + (dx < 0)
+        return 3 + (kind * CHUNKS + c) * 2 + (dx < 0)
 
     def fold_core():
         return remote(0, big.at[edge, core_edge], from_c, gx, partner)
@@ -207,11 +214,13 @@
         rs = slice(c * depth_of, (c + 1) * depth_of)
         return remote(numbered(1, c, dx), big.at[piece(beyond[dx], c), far_edge], from_d.at[int(dx < 0), rs], gx + dx, outer)
 
-    def halo_partner():
-        return remote(3, win.at[mid, core_near], win.at[mid, far_edge], gx, partner)
-
-    def halo_outer():
-        return remote(4, win.at[mid, far_near], win.at[mid, core_edge], gx, outer)
+    def halo_partner(c, dx):
+        rs = piece(lands[dx], c)
+        return remote(numbered(5, c, dx), win.at[rs, core_near], win.at[rs, far_edge], gx, partner)
+
+    def halo_outer(c, dx):
+        rs = piece(lands[dx], c)
+        return remote(numbered(6, c, dx), win.at[rs, far_near], win.at[rs, core_edge], gx, outer)
 
     def halo_x(c, dx):
         return remote(numbered(2, c, dx), win.at[piece(near[dx], c), mid], win.at[piece(far[dx], c), mid], gx + dx, gy)
@@ -229,24 +238,33 @@
     def back(rs, cs):
         big[rs, cs] = product(part(trans, rs, every), part(work, every, cs))
 
+    for load in loads[layers + 6 : layers + 10]:
+        load.wait()
     mix(edge)
     back(edge, edge)
     sides = 2 - (gx == 0).astype(jnp.int32) - (gx == nx - 1).astype(jnp.int32)
     pl.semaphore_wait(barrier, (sides + 1) * jnp.where(has_outer, 2, 1))
     fold_core().start()
-    for c, dx in each:
-        only_if(there(dx) & has_outer, lambda: fold_d(c, dx).start())
+    for dx in steps:
+        only_if(there(dx) & has_outer, lambda: fold_d(0, dx).start())
     mix(mid)
     back(edge, mid)
     fold_core().wait_recv()
     big[edge, core_near] = big[edge, core_near] + from_c[...]
-    for c, dx in each:
-        only_if(there(dx), lambda: fold_x(c, dx).start())
+    for dx in steps:
+        only_if(there(dx), lambda: fold_x(0, dx).start())
     back(mid, edge)
     fold_partner().start()
     only_if(has_outer, lambda: fold_outer().start())
+    for c in range(1, CHUNKS):
+        for dx in steps:
+            @pl.when(there(dx))
+            def _():
+                fold_x(c, dx).start()
+
+            only_if(there(dx) & has_outer, lambda: fold_d(c, dx).start())
     back(mid, mid)
-    for load in loads[7:]:
+    for load in loads[layers + 10 :]:
         load.wait()
 
     fold_partner().wait_recv()
@@ -276,14 +294,15 @@
         win[rs, mid] = sta[tile_rows, :].astype(F32) * (ahead - obs[tile_rows, :])
         only_if(there(-dx), lambda: halo_x(c, -dx).start())
         only_if(there(-dx) & has_outer, lambda: halo_d(c, -dx).start())
-
-    halo_partner().start()
-    only_if(has_outer, lambda: halo_outer().start())
+        halo_partner(c, dx).start()
+        only_if(has_outer, lambda: halo_outer(c, dx).start())
+
     predicted[...] = big[mid, mid]
     residual[...] = win[mid, mid]
 
-    halo_partner().wait_recv()
-    only_if(has_outer, lambda: halo_outer().wait_recv())
+    for c, dx in each:
+        halo_partner(c, dx).wait_recv()
+        only_if(has_outer, lambda: halo_outer(c, dx).wait_recv())
     put(work, mid, every, product(split(win[mid, :]), part(trans, every, every)))
     for band in bands:
         total[band, :] = product(part(basis, band, mid), part(work, mid, every))
@@ -304,14 +323,11 @@
 
     fold_core().wait_send()
     fold_partner().wait_send()
-    halo_partner().wait_send()
-
-    @pl.when(has_outer)
-    def _():
-        fold_outer().wait_send()
-        halo_outer().wait_send()
-
+    only_if(has_outer, lambda: fold_outer().wait_send())
     for c, dx in each:
+        halo_partner(c, dx).wait_send()
+        only_if(has_outer, lambda: halo_outer(c, dx).wait_send())
+
         @pl.when(there(dx))
         def _():
             fold_x(c, dx).wait_send()
@@ -335,7 +351,7 @@
     half = length // 2
     mid, every, own = slice(2 * RADIUS, length), slice(0, length), slice(0, tile)
     bands = [slice(r * half, (r + 1) * half) for r in range(2)]
-    basis, trans, mixed, work = (b_h, b_l), (t_h, t_l), (z_h, z_l), (w_h, w_l)
+    basis, trans = (b_h, b_l), (t_h, t_l)
     stores = [
         pltpu.make_async_copy(predicted, predicted_out, out_sem.at[0]),
         pltpu.make_async_copy(residual, residual_out, out_sem.at[1]),
@@ -344,15 +360,20 @@
         store.start()
     for layer in range(layers):
         spectrum = spectra[layer]
+        mixed, work = (z_h.at[layer], z_l.at[layer]), (w_h.at[layer], w_l.at[layer])
         for band in bands:
             for at in bands:
                 put(mixed, band, at, spectrum * blocks[band, at])
-        for band in bands:
             put(work, band, own, product(part(mixed, band, every), part(basis, every, mid)))
-        grad[layer] = product(part(trans, mid, every), part(work, every, own))
-        store = pltpu.make_async_copy(grad.at[layer], gradient.at[layer], out_sem.at[2 + layer])
-        store.start()
-        stores.append(store)
+    for layer in range(layers):
+        work = (w_h.at[layer], w_l.at[layer])
+        for n in range(2):
+            rs = slice(n * RADIUS, (n + 1) * RADIUS)
+            inner = slice(mid.start + n * RADIUS, mid.start + (n + 1) * RADIUS)
+            grad[layer, rs] = product(part(trans, inner, every), part(work, every, own))
+            store = pltpu.make_async_copy(grad.at[layer, rs], gradient.at[layer, rs], out_sem.at[2 + 2 * layer + n])
+            store.start()
+            stores.append(store)
     for store in stores:
         store.wait()
 
@@ -394,9 +415,9 @@
                 pltpu.VMEM((2, RADIUS, RADIUS), F32),
                 pltpu.SMEM((layers,), jnp.int32),
                 pltpu.SemaphoreType.DMA,
-                pltpu.SemaphoreType.DMA((9,)),
-                pltpu.SemaphoreType.DMA((5 + 10 * CHUNKS,)),
-                pltpu.SemaphoreType.DMA((5 + 10 * CHUNKS,)),
+                pltpu.SemaphoreType.DMA((layers + 12,)),
+                pltpu.SemaphoreType.DMA((3 + 14 * CHUNKS,)),
+                pltpu.SemaphoreType.DMA((3 + 14 * CHUNKS,)),
             ],
             compiler_params=pltpu.CompilerParams(
                 collective_id=0, has_side_effects=True, vmem_limit_bytes=32 << 20
@@ -413,11 +434,12 @@
             in_specs=[vmem] * 8,
             out_specs=(anywhere,) * 3,
             scratch_shapes=[
-                wide, wide,
-                pltpu.VMEM((length, tile), BF16),
-                pltpu.VMEM((length, tile), BF16),
+                pltpu.VMEM((layers, length, length), BF16),
+                pltpu.VMEM((layers, length, length), BF16),
+                pltpu.VMEM((layers, length, tile), BF16),
+                pltpu.VMEM((layers, length, tile), BF16),
                 pltpu.VMEM((layers, tile, tile), F32),
-                pltpu.SemaphoreType.DMA((2 + layers,)),
+                pltpu.SemaphoreType.DMA((2 + 2 * layers,)),
             ],
             compiler_params=pltpu.CompilerParams(vmem_limit_bytes=24 << 20),
             name="adjoint",

time: 38.7 us -> 37.9 us (0.979)
  Pallas kernels: 38 us -> 37.2 us
    pallas_call x1, Pallas kernels: 2.73 us -> 2.18 us  [body(): pl.pallas_call(adjoint_kernel, out_shape=(jax.ShapeDtypeStruct((tile, til...]
where the time goes in v4:
time: 37.9 us; the launch traced here: 37.8 us
  Pallas kernels  37.2 us (98%)
  between operations  0.64 us (2%)
    pallas_call x1, Pallas kernels, body(): pl.pallas_call(functools.partial(forward_kernel, counts), out_shape=(pltp...  35 us
    pallas_call x1, Pallas kernels, body(): pl.pallas_call(adjoint_kernel, out_shape=(jax.ShapeDtypeStruct((tile, til...  2.18 us

profile of v4, /device:TPU:57, one launch (start us, length us, event | category | flops | bytes accessed | tf_op | source)
XLA Modules:
  0.0 37.8 jit_solution(548270419018425732)
XLA Ops:
  0.6 35.0 %forward.1 = (f32[256,256]{1,0:T(8,128)S(1)}, f32[256,256]{1,0:T(8,128)S(1)}, f32[512,512]{1,0:T(8,128)S(1)}, f32[2,256,256]{2,1,0:T(8,128)S(1)}, bf16[512,512]{...) custom-call(s32[2]{0:T(128)} %layer_index.1, ...), custom_call_target="tpu_custom_call" | custom-call | tf_op jit(solution)/shard_map/forward/pallas_call | solution.py:394
  35.7 2.2 %adjoint.1 = (f32[256,256]{1,0:T(8,128)}, f32[256,256]{1,0:T(8,128)}, f32[2,256,256]{2,1,0:T(8,128)}) custom-call(f32[256,256]{1,0:T(8,128)S(1)} %get-tuple-element.11.predicted, f32[256,256]{1,0:T(8,128)S(1)} %get-tuple-element.12.residual, f32[512,512]{1,0:T(8,128)S(1)} %get-tuple-element.13.blocks, f32[2,256,256]{2,1,0:T(8,128)S(1)} %get-tuple-element.14.spectra, ...), custom_call_target="tpu_custom_call" | custom-call | tf_op jit(solution)/shard_map/adjoint/pallas_call | solution.py:427

commit v5 on v4

--- a/solution.py
+++ b/solution.py
@@ -107,10 +107,11 @@
     def greet(x, y):
         pl.semaphore_signal(barrier, inc=1, device_id={"gx": x, "gy": y}, device_id_type=MESH)
 
+    only_if(has_outer, lambda: greet(gx, outer))
     greet(gx, partner)
-    only_if(has_outer, lambda: greet(gx, outer))
     for dx in steps:
         only_if(there(dx), lambda: greet(gx + dx, gy))
+    for dx in steps:
         only_if(there(dx) & has_outer, lambda: greet(gx + dx, outer))
 
     pairs = [(cos_h, c_h), (cos_l, c_l)]
@@ -245,25 +246,18 @@
     sides = 2 - (gx == 0).astype(jnp.int32) - (gx == nx - 1).astype(jnp.int32)
     pl.semaphore_wait(barrier, (sides + 1) * jnp.where(has_outer, 2, 1))
     fold_core().start()
-    for dx in steps:
-        only_if(there(dx) & has_outer, lambda: fold_d(0, dx).start())
+    for c, dx in each:
+        only_if(there(dx) & has_outer, lambda: fold_d(c, dx).start())
     mix(mid)
     back(edge, mid)
     fold_core().wait_recv()
     big[edge, core_near] = big[edge, core_near] + from_c[...]
-    for dx in steps:
-        only_if(there(dx), lambda: fold_x(0, dx).start())
+    for c, dx in each:
+        only_if(there(dx), lambda: fold_x(c, dx).start())
     back(mid, edge)
+    back(mid, mid)
     fold_partner().start()
     only_if(has_outer, lambda: fold_outer().start())
-    for c in range(1, CHUNKS):
-        for dx in steps:
-            @pl.when(there(dx))
-            def _():
-                fold_x(c, dx).start()
-
-            only_if(there(dx) & has_outer, lambda: fold_d(c, dx).start())
-    back(mid, mid)
     for load in loads[layers + 10 :]:
         load.wait()
 
@@ -307,6 +301,13 @@
     for band in bands:
         total[band, :] = product(part(basis, band, mid), part(work, mid, every))
 
+    fold_core().wait_send()
+    fold_partner().wait_send()
+    only_if(has_outer, lambda: fold_outer().wait_send())
+    for c, dx in each:
+        only_if(there(dx), lambda: fold_x(c, dx).wait_send())
+        only_if(there(dx) & has_outer, lambda: fold_d(c, dx).wait_send())
+
     for c, dx in each:
         @pl.when(there(-dx))
         def _():
@@ -314,6 +315,12 @@
             halo_core(c, dx).start()
 
     wait_x[...] = product(split(win[edge, mid]), part(trans, mid, every))
+    for c, dx in each:
+        halo_partner(c, dx).wait_send()
+        only_if(has_outer, lambda: halo_outer(c, dx).wait_send())
+        only_if(there(dx), lambda: halo_x(c, dx).wait_send())
+        only_if(there(dx) & has_outer, lambda: halo_d(c, dx).wait_send())
+
     for c, dx in each:
         only_if(there(-dx), lambda: halo_core(c, dx).wait_recv())
         only_if(there(-dx) & has_outer, lambda: halo_d(c, dx).wait_recv())
@@ -321,23 +328,7 @@
     for band in bands:
         blocks[band, :] = total[band, :] + product(part(basis, band, edge), part(work, edge, every))
 
-    fold_core().wait_send()
-    fold_partner().wait_send()
-    only_if(has_outer, lambda: fold_outer().wait_send())
-    for c, dx in each:
-        halo_partner(c, dx).wait_send()
-        only_if(has_outer, lambda: halo_outer(c, dx).wait_send())
-
-        @pl.when(there(dx))
-        def _():
-            fold_x(c, dx).wait_send()
-            halo_x(c, dx).wait_send()
-
-        @pl.when(there(dx) & has_outer)
-        def _():
-            fold_d(c, dx).wait_send()
-            halo_d(c, dx).wait_send()
-
+    for c, dx in each:
         only_if(there(-dx), lambda: halo_core(c, dx).wait_send())
 
 

time: 37.9 us -> 37.9 us (level)
  no operation moved by 1% of the time
where the time goes in v5:
time: 37.9 us; the launch traced here: 37.8 us
  Pallas kernels  37.2 us (98%)
  between operations  0.64 us (2%)
    pallas_call x1, Pallas kernels, body(): pl.pallas_call(functools.partial(forward_kernel, counts), out_shape=(pltp...  35 us
    pallas_call x1, Pallas kernels, body(): pl.pallas_call(adjoint_kernel, out_shape=(jax.ShapeDtypeStruct((tile, til...  2.18 us

profile of v5, /device:TPU:57, one launch (start us, length us, event | category | flops | bytes accessed | tf_op | source)
XLA Modules:
  0.0 37.8 jit_solution(5118674345650416438)
XLA Ops:
  0.6 35.0 %forward.1 = (f32[256,256]{1,0:T(8,128)S(1)}, f32[256,256]{1,0:T(8,128)S(1)}, f32[512,512]{1,0:T(8,128)S(1)}, f32[2,256,256]{2,1,0:T(8,128)S(1)}, bf16[512,512]{...) custom-call(s32[2]{0:T(128)} %layer_index.1, ...), custom_call_target="tpu_custom_call" | custom-call | tf_op jit(solution)/shard_map/forward/pallas_call | solution.py:385
  35.6 2.2 %adjoint.1 = (f32[256,256]{1,0:T(8,128)}, f32[256,256]{1,0:T(8,128)}, f32[2,256,256]{2,1,0:T(8,128)}) custom-call(f32[256,256]{1,0:T(8,128)S(1)} %get-tuple-element.11.predicted, f32[256,256]{1,0:T(8,128)S(1)} %get-tuple-element.12.residual, f32[512,512]{1,0:T(8,128)S(1)} %get-tuple-element.13.blocks, f32[2,256,256]{2,1,0:T(8,128)S(1)} %get-tuple-element.14.spectra, ...), custom_call_target="tpu_custom_call" | custom-call | tf_op jit(solution)/shard_map/adjoint/pallas_call | solution.py:418
